TPU v7x, 32 devices: a whole 2x2x4 slice. The times are simulated.
32 devices in a mesh: slides: 2 (over y), tile: 4 (over z), col: 2 (over x), mp: 2 (over core).
Axes of the slice: x: 2, y: 2, z: 4, core: 2. Of those that a mesh axis runs over, the one named last changes fastest.
Arguments:
- patches: bfloat16 [128, 48, 1024], P(('slides', 'tile'), 'col', 'mp'), parts along dimension 0, may hold values from -8 to 8
- tissue: int32 [128, 48], P(('slides', 'tile'), 'col'), parts along dimension 0, may hold values from 0 to 1, as said below
- conv_weight: bfloat16 [3, 3, 1024], P(None, None, 'mp'), may hold values from -2 to 2
- ln_gain: float32 [1024], P('mp'), may hold values from 0.1 to 1.9
- qkv_weight: bfloat16 [3, 1024, 1024], P(None, None, 'mp'), may hold values from -0.1875 to 0.1875
- omega: float32 [256, 64], replicated, may hold values from -6 to 6
- out_weight: bfloat16 [1024, 1024], P('mp'), may hold values from -0.1875 to 0.1875
Outputs:
- layer_out: bfloat16 [128, 48, 1024], P(('slides', 'tile'), 'col', 'mp'), parts along dimension 0
There are 2 independent parts, one for each index of `slides`. A program takes and returns all parts, laid end to end along the dimension named above; an argument that names none is the same for every part. Nothing has to cross between parts.
Inputs may be any that keep to these rules, and one draw needn't show every extreme that they name: 1 marks tissue, 0 background; the slide's first patch is tissue.
All inputs are finite; a program needn't handle non-finite values.
Results may differ from a plain program's by a relative error of at most 0.0065.
Values may be sent and summed in bfloat16 or wider, within the bound.
A program may use at most 64 MiB of HBM per device.

v0:
```python
import math
import jax
import jax.numpy as jnp
from jax import lax
from jax.sharding import PartitionSpec as P

E = 64
M = 256


def extended(cells, sides, width):
    for axis, dim in sides:
        count = lax.axis_size(axis)
        ends = count - 1
        head = lax.slice_in_dim(cells, 0, width, axis=dim)
        tail = lax.slice_in_dim(cells, cells.shape[dim] - width, cells.shape[dim], axis=dim)
        cells = jnp.concatenate(
            [
                lax.ppermute(tail, axis, [(i, (i + 1) % count) for i in range(ends)]),
                cells,
                lax.ppermute(head, axis, [((i + 1) % count, i) for i in range(ends)]),
            ],
            axis=dim,
        )
    return cells


def features(scaled, omega):
    lifted = jnp.einsum("the,me->thm", scaled, omega, precision=lax.Precision.HIGHEST)
    square = 0.5 * jnp.sum(scaled * scaled, axis=-1, keepdims=True)
    return (jnp.exp(lifted - square) / math.sqrt(M)).astype(jnp.bfloat16)


def split_pair(values):
    upper = values.astype(jnp.bfloat16)
    lower = (values - upper.astype(jnp.float32)).astype(jnp.bfloat16)
    return (upper, lower)


def shards(patches, tissue, conv_weight, ln_gain, qkv_weight, omega, out_weight):
    rows_here, cols_here, half = patches.shape
    tokens = rows_here * cols_here
    padded = extended(patches, (("tile", 0), ("col", 1)), 1)
    widened = padded.astype(jnp.float32)
    kernel = conv_weight.astype(jnp.float32)
    stem = patches.astype(jnp.float32)
    for row_off in range(3):
        for col_off in range(3):
            stem = (
                stem
                + kernel[row_off, col_off]
                * widened[row_off : row_off + rows_here, col_off : col_off + cols_here]
            )
    flat = stem.reshape(tokens, half)
    totals = lax.psum((jnp.sum(flat, axis=1), jnp.sum(flat * flat, axis=1)), "mp")
    width = half * lax.axis_size("mp")
    mean_val = totals[0] / width
    var_val = totals[1] / width - mean_val * mean_val
    normed = ((flat - mean_val[:, None]) * lax.rsqrt(var_val + 1e-05)[:, None] * ln_gain).astype(
        jnp.bfloat16
    )
    projected = jnp.einsum(
        "td,cdf->ctf",
        lax.all_gather(normed, "mp", axis=1, tiled=True),
        qkv_weight,
        preferred_element_type=jnp.float32,
    ).astype(jnp.bfloat16)
    heads_here = qkv_weight.shape[2] // E
    scale = E ** (-0.25)
    key_part = projected[1].astype(jnp.float32).reshape(tokens, heads_here, E) * scale
    keep = tissue.reshape(tokens).astype(jnp.bfloat16)
    key_feat = features(key_part, omega) * keep[:, None, None]
    value_part = projected[2].reshape(tokens, heads_here, E)
    state = jnp.einsum("the,thm->hem", value_part, key_feat, preferred_element_type=jnp.float32)
    key_sum = jnp.sum(key_feat.astype(jnp.float32), axis=0)
    kv_state, normalizer = lax.psum((state, key_sum), ("tile", "col"))
    query_part = projected[0].astype(jnp.float32).reshape(tokens, heads_here, E) * scale
    query_feat = features(query_part, omega)
    state_upper, state_lower = split_pair(kv_state)
    norm_upper, norm_lower = split_pair(normalizer)
    numer = jnp.einsum("thm,hem->the", query_feat, state_upper, preferred_element_type=jnp.float32)
    numer = numer + jnp.einsum(
        "thm,hem->the", query_feat, state_lower, preferred_element_type=jnp.float32
    )
    denom = jnp.einsum("thm,hm->th", query_feat, norm_upper, preferred_element_type=jnp.float32)
    denom = denom + jnp.einsum(
        "thm,hm->th", query_feat, norm_lower, preferred_element_type=jnp.float32
    )
    attended = (numer / denom[:, :, None]).astype(jnp.bfloat16).reshape(tokens, heads_here * E)
    mixed = (
        lax.psum_scatter(
            lax.dot_general(
                out_weight, attended, (((0,), (1,)), ((), ())), preferred_element_type=jnp.float32
            ).astype(jnp.bfloat16),
            "mp",
            scatter_dimension=0,
            tiled=True,
        )
        .astype(jnp.float32)
        .T
    )
    return (flat + mixed).astype(jnp.bfloat16).reshape(rows_here, cols_here, half)


def solution(mesh):
    placed = (
        P(("slides", "tile"), "col", "mp"),
        P(("slides", "tile"), "col"),
        P(None, None, "mp"),
        P("mp"),
        P(None, None, "mp"),
        P(),
        P("mp", None),
    )
    return jax.shard_map(
        shards,
        mesh=mesh,
        in_specs=placed,
        out_specs=P(("slides", "tile"), "col", "mp"),
        check_vma=False,
    )
```

profile of v0, /device:TPU:0, one launch (start us, length us, event | category | flops | bytes accessed | tf_op | source)
XLA Modules:
  0.0 167.3 jit_solution(4556089762340972274)
XLA Ops:
  7.5 5.0 %collective-permute-start = (bf16[1,24,512]{2,1,0:T(8,128)(2,1)S(1)}, bf16[1,24,512]{2,1,0:T(8,128)(2,1)S(1)}, u32[]{:S(2)}, u32[]{:S(2)}) collective-permute-start(bf16[1,24,512]{2,1,0:T(8,128)(2,1)S(1)} %get-tuple-element.15), channel_id=1, source_target_pairs={{0,4},{4,8},{8,12},{1,5},{5,9},{9,13},{2,6},{6,10},{10,14},{3,7},{... | collective-permute-start | bytes 73736 | tf_op jit(solution)/shard_map/ppermute | solution.py:19
  12.5 1.3 collective-permute-start.1
  15.0 3.2 %collective-permute-done.1 = bf16[1,24,512]{2,1,0:T(8,128)(2,1)S(1)} collective-permute-done((bf16[1,24,512]{2,1,0:T(8,128)(2,1)S(1)}, bf16[1,24,512]{2,1,0:T(8,128)(2,1)S(1)}, u32[]{:S(2)}, u32[]{:S(2)}) %collective-permute-start.1) | collective-permute-done | bytes 24608 | tf_op jit(solution)/shard_map/ppermute | solution.py:21
  19.7 4.0 %collective-permute-start.2 = (bf16[18,1,512]{2,1,0:T(2,128)(2,1)}, bf16[18,1,512]{2,1,0:T(2,128)(2,1)}, u32[]{:S(2)}, u32[]{:S(2)}) collective-permute-start(bf16[18,1,512]{2,1,0:T(2,128)(2,1)} %get-tuple-element.12), channel_id=1, source_target_pairs={{0,2},{1,3},{4,6},{5,7},{8,10},{9,11},{12,14},{13,15},{16,18},{17,... | collective-permute-start | bytes 55304 | tf_op jit(solution)/shard_map/ppermute | solution.py:19
  23.7 1.3 collective-permute-start.3
  25.0 1.5 fusion.35
  27.9 2.0 %collective-permute-done.3 = bf16[18,1,512]{2,1,0:T(2,128)(2,1)} collective-permute-done((bf16[18,1,512]{2,1,0:T(2,128)(2,1)}, bf16[18,1,512]{2,1,0:T(2,128)(2,1)}, u32[]{:S(2)}, u32[]{:S(2)}) %collective-permute-start.3) | collective-permute-done | bytes 18464 | tf_op jit(solution)/shard_map/ppermute | solution.py:21
  31.2 1.7 %fusion.31 = (f32[16,24]{1,0:T(8,128)S(1)}, f32[16,24]{1,0:T(8,128)S(1)}, f32[16,24,512]{2,1,0:T(8,128)}) fusion(f32[18,26,512]{2,1,0:T(8,128)S(1)} %maximum_convert_fusion, f32[512]{0:T(512)S(1)} %bitcast.83, f32[512]{0:T(512)S(1)} %bitcast.82, f32[512]{0:T(512)S(1)} %bitcast.81, f32[512]{0:T(512)S(1)} %bitcast.80, f32[512]{0:T(512)S(1)} %bitcast.79, ...), kind=kLoop, calls=%fused_computation.65 | loop fusion | flops 4324608 | bytes 8279040 | tf_op jit(solution)/shard_map/reduce_sum | solution.py:55
  33.1 2.5 %all-reduce = (f32[384]{0:T(512)S(1)}, f32[384]{0:T(512)S(1)}) all-reduce(f32[384]{0:T(512)S(1)} %reduce_sum.52, f32[384]{0:T(512)S(1)} %reduce_sum.50), channel_id=1, replica_groups=mesh['slides'=2,'tile'=4,'col'=2,'mp'=2] {'mp'}, use_global_device_ids=true, to_apply=%region_3.0 | all-reduce | flops 768 | bytes 6144 | tf_op jit(solution)/shard_map/psum | solution.py:55
  35.6 1.3 fusion.19
  36.9 2.4 %all_gather.3 = bf16[384,1024]{1,0:T(8,128)(2,1)S(1)} all-gather(bf16[384,512]{1,0:T(8,128)(2,1)S(1)} %fusion.19), channel_id=1, replica_groups=mesh['slides'=2,'tile'=4,'col'=2,'mp'=2] {'mp'}, dimensions={1}, use_global_device_ids=true | all-gather | bytes 1179648 | tf_op jit(solution)/shard_map/all_gather | solution.py:64
  39.3 1.4 fusion.1
  41.4 1.4 convert_multiply_fusion.1
  44.0 2.3 %copy.12 = f32[1,384,512]{1,2,0:T(8,128)} copy(f32[1,384,512]{2,1,0:T(8,128)} %get-tuple-element.10) | data formatting | bytes 1572864 | tf_op jit(solution)/shard_map/mul | solution.py:70
  47.6 5.8 %convert_reduce_fusion = (f32[8,256]{1,0:T(8,128)S(1)}, bf16[384,8,256]{2,0,1:T(8,128)(2,1)}) fusion(bf16[384]{0:T(512)(128)(2,1)S(1)} %copy-done.15, f32[384,8]{0,1:T(8,128)S(1)} %broadcast_multiply_fusion.1, f32[384,8,64]{0,2,1:T(8,128)} %bitcast.71, f32[256,64]{0,1:T(8,128)} %param.12), kind=kOutput, calls=%fused_computation | convolution fusion | flops 608696320 | bytes 2446080 | tf_op jit(solution)/shard_map/the,me->thm/dot_general | solution.py:29
  53.3 19.8 %psum.31 = f32[8,256]{1,0:T(8,128)S(1)} all-reduce(f32[8,256]{1,0:T(8,128)S(1)} %get-tuple-element.29), channel_id=1, replica_groups=mesh['slides'=2,'tile'=4,'col'=2,'mp'=2] {'tile','col'}, use_global_device_ids=true, to_apply=%region_8.0 | all-reduce | flops 2048 | bytes 16384 | tf_op jit(solution)/shard_map/psum | solution.py:76
  73.1 2.6 %fusion.36 = f32[8,64,256]{2,1,0:T(8,128)} fusion(bf16[384,8,64]{0,2,1:T(8,128)(2,1)S(1)} %bitcast.74, bf16[384,8,256]{2,0,1:T(8,128)(2,1)} %get-tuple-element.30), kind=kOutput, calls=%fused_computation.69 | convolution fusion | flops 100663296 | bytes 2490368 | tf_op jit(solution)/shard_map/the,thm->hem/dot_general | solution.py:74
  76.0 2.3 %copy.13 = f32[1,384,512]{1,2,0:T(8,128)} copy(f32[1,384,512]{2,1,0:T(8,128)} %get-tuple-element.11) | data formatting | bytes 1572864 | tf_op jit(solution)/shard_map/mul | solution.py:77
  79.5 4.4 %multiply_convert_fusion = bf16[384,8,256]{2,0,1:T(8,128)(2,1)S(1)} fusion(f32[384,8,64]{0,2,1:T(8,128)} %bitcast.73, f32[384,8]{0,1:T(8,128)S(1)} %broadcast_multiply_fusion, f32[256,64]{0,1:T(8,128)S(1)} %copy-done.17), kind=kOutput, calls=%fused_computation.1 | convolution fusion | flops 606339072 | bytes 2437120 | tf_op jit(solution)/shard_map/the,me->thm/dot_general | solution.py:29
  85.0 60.6 %all-reduce.3.cloned.1.call-done = f32[8,64,256]{2,1,0:T(8,128)} async-done(((f32[8,64,256]{2,1,0:T(8,128)}), f32[8,64,256]{2,1,0:T(8,128)}) %all-reduce.3.cloned.1.call-update) | async-done | bytes 524304 | tf_op jit(solution)/shard_map/psum | solution.py:76
  145.6 2.3 %fusion.21 = f32[8,64,384]{2,1,0:T(8,128)S(1)} fusion(bf16[384,8,256]{2,0,1:T(8,128)(2,1)} %copy-done.1, f32[8,64,256]{2,1,0:T(8,128)} %all-reduce.3.cloned.1.call-done), kind=kOutput, calls=%fused_computation.45 | convolution fusion | flops 100794368 | bytes 2883584 | tf_op jit(solution)/shard_map/thm,hem->the/dot_general | solution.py:81
  149.2 1.5 fusion.2
  150.7 7.7 %reduce-scatter.2.cloned.1.call-done = bf16[512,384]{0,1:T(8,128)(2,1)} async-done(((bf16[1024,384]{0,1:T(8,128)(2,1)}), bf16[512,384]{0,1:T(8,128)(2,1)}) %reduce-scatter.2.cloned.1.call-update) | async-done | bytes 393232 | tf_op jit(solution)/shard_map/reduce_scatter | solution.py:91
  158.3 2.1 %fusion.15 = bf16[384,512]{1,0:T(8,128)(2,1)} fusion(f32[16,24,512]{2,1,0:T(8,128)} %get-tuple-element.9, bf16[512,384]{0,1:T(8,128)(2,1)} %reduce-scatter.2.cloned.1.call-done), kind=kLoop, calls=%fused_computation.31 | loop fusion | flops 589824 | bytes 1572864 | tf_op jit(solution)/shard_map/convert_element_type | solution.py:102
  (64 shorter events, 13.4 us)
Async XLA Ops:
  6.5 32.7 %copy-start = (bf16[3,1024,512]{2,1,0:T(8,128)(2,1)S(1)}, bf16[3,1024,512]{2,1,0:T(8,128)(2,1)}, u32[]{:S(2)}) copy-start(bf16[3,1024,512]{2,1,0:T(8,128)(2,1)} %param.11) | copy-start | bytes 9437188
  6.5 24.6 %copy-start.3 = (bf16[16,24,512]{2,1,0:T(8,128)(2,1)S(1)}, bf16[16,24,512]{2,1,0:T(8,128)(2,1)}, u32[]{:S(2)}) copy-start(bf16[16,24,512]{2,1,0:T(8,128)(2,1)} %param.7) | copy-start | bytes 1179652
  6.5 139.1 %all-reduce.3.cloned.1.call-start = ((), (), s32[]{:S(2)}) async-start(), calls=%async_computation.1 | async-start | bytes 1048576 | tf_op jit(solution)/shard_map/psum | solution.py:76
  7.5 6.6 %collective-permute-start = (bf16[1,24,512]{2,1,0:T(8,128)(2,1)S(1)}, bf16[1,24,512]{2,1,0:T(8,128)(2,1)S(1)}, u32[]{:S(2)}, u32[]{:S(2)}) collective-permute-start(bf16[1,24,512]{2,1,0:T(8,128)(2,1)S(1)} %get-tuple-element.15), channel_id=1, source_target_pairs={{0,4},{4,8},{8,12},{1,5},{5,9},{9,13},{2,6},{6,10},{10,14},{3,7},{... | collective-permute-start | bytes 73736 | tf_op jit(solution)/shard_map/ppermute | solution.py:19
  12.5 5.7 %collective-permute-start.1 = (bf16[1,24,512]{2,1,0:T(8,128)(2,1)S(1)}, bf16[1,24,512]{2,1,0:T(8,128)(2,1)S(1)}, u32[]{:S(2)}, u32[]{:S(2)}) collective-permute-start(bf16[1,24,512]{2,1,0:T(8,128)(2,1)S(1)} %get-tuple-element.14), channel_id=1, source_target_pairs={{4,0},{8,4},{12,8},{5,1},{9,5},{13,9},{6,2},{10,6},{14,10},{7,3},{... | collective-permute-start | bytes 73736 | tf_op jit(solution)/shard_map/ppermute | solution.py:21
  18.2 0.8 copy-start.4
  19.7 8.2 %collective-permute-start.2 = (bf16[18,1,512]{2,1,0:T(2,128)(2,1)}, bf16[18,1,512]{2,1,0:T(2,128)(2,1)}, u32[]{:S(2)}, u32[]{:S(2)}) collective-permute-start(bf16[18,1,512]{2,1,0:T(2,128)(2,1)} %get-tuple-element.12), channel_id=1, source_target_pairs={{0,2},{1,3},{4,6},{5,7},{8,10},{9,11},{12,14},{13,15},{16,18},{17,... | collective-permute-start | bytes 55304 | tf_op jit(solution)/shard_map/ppermute | solution.py:19
  23.7 6.2 %collective-permute-start.3 = (bf16[18,1,512]{2,1,0:T(2,128)(2,1)}, bf16[18,1,512]{2,1,0:T(2,128)(2,1)}, u32[]{:S(2)}, u32[]{:S(2)}) collective-permute-start(bf16[18,1,512]{2,1,0:T(2,128)(2,1)} %get-tuple-element.13), channel_id=1, source_target_pairs={{2,0},{3,1},{6,4},{7,5},{10,8},{11,9},{14,12},{15,13},{18,16},{19,... | collective-permute-start | bytes 55304 | tf_op jit(solution)/shard_map/ppermute | solution.py:21
  27.8 3.3 %copy-start.6 = (f32[1,1,512]{2,1,0:T(1,128)S(1)}, f32[1,1,512]{2,1,0:T(1,128)}, u32[]{:S(2)}) copy-start(f32[1,1,512]{2,1,0:T(1,128)} %get-tuple-element.16) | copy-start | bytes 6148
  27.8 3.3 %copy-start.7 = (f32[1,1,512]{2,1,0:T(1,128)S(1)}, f32[1,1,512]{2,1,0:T(1,128)}, u32[]{:S(2)}) copy-start(f32[1,1,512]{2,1,0:T(1,128)} %get-tuple-element.17) | copy-start | bytes 6148
  27.8 3.3 %copy-start.8 = (f32[1,1,512]{2,1,0:T(1,128)S(1)}, f32[1,1,512]{2,1,0:T(1,128)}, u32[]{:S(2)}) copy-start(f32[1,1,512]{2,1,0:T(1,128)} %get-tuple-element.18) | copy-start | bytes 6148
  27.8 3.3 %copy-start.9 = (f32[1,1,512]{2,1,0:T(1,128)S(1)}, f32[1,1,512]{2,1,0:T(1,128)}, u32[]{:S(2)}) copy-start(f32[1,1,512]{2,1,0:T(1,128)} %get-tuple-element.19) | copy-start | bytes 6148
  27.8 3.4 %copy-start.10 = (f32[1,1,512]{2,1,0:T(1,128)S(1)}, f32[1,1,512]{2,1,0:T(1,128)}, u32[]{:S(2)}) copy-start(f32[1,1,512]{2,1,0:T(1,128)} %get-tuple-element.20) | copy-start | bytes 6148
  27.8 3.4 %copy-start.11 = (f32[1,1,512]{2,1,0:T(1,128)S(1)}, f32[1,1,512]{2,1,0:T(1,128)}, u32[]{:S(2)}) copy-start(f32[1,1,512]{2,1,0:T(1,128)} %get-tuple-element.21) | copy-start | bytes 6148
  27.8 3.4 %copy-start.12 = (f32[1,1,512]{2,1,0:T(1,128)S(1)}, f32[1,1,512]{2,1,0:T(1,128)}, u32[]{:S(2)}) copy-start(f32[1,1,512]{2,1,0:T(1,128)} %get-tuple-element.22) | copy-start | bytes 6148
  27.8 3.4 %copy-start.13 = (f32[1,1,512]{2,1,0:T(1,128)S(1)}, f32[1,1,512]{2,1,0:T(1,128)}, u32[]{:S(2)}) copy-start(f32[1,1,512]{2,1,0:T(1,128)} %get-tuple-element.23) | copy-start | bytes 6148
  27.8 3.4 %copy-start.14 = (f32[1,1,512]{2,1,0:T(1,128)S(1)}, f32[1,1,512]{2,1,0:T(1,128)}, u32[]{:S(2)}) copy-start(f32[1,1,512]{2,1,0:T(1,128)} %get-tuple-element.24) | copy-start | bytes 6148
  42.8 4.7 %copy-start.15 = (bf16[384]{0:T(512)(128)(2,1)S(1)}, bf16[384]{0:T(512)(128)(2,1)}, u32[]{:S(2)}) copy-start(bf16[384]{0:T(512)(128)(2,1)} %convert_element_type.95) | copy-start | bytes 2308
  75.7 3.8 %copy-start.17 = (f32[256,64]{0,1:T(8,128)S(1)}, f32[256,64]{0,1:T(8,128)}, u32[]{:S(2)}) copy-start(f32[256,64]{0,1:T(8,128)} %param.12) | copy-start | bytes 196612
  75.7 82.6 %reduce-scatter.2.cloned.1.call-start = ((), (), s32[]{:S(2)}) async-start(), calls=%async_computation.2 | async-start | bytes 1179648 | tf_op jit(solution)/shard_map/reduce_scatter | solution.py:91
  83.9 1.2 copy-start.1
  145.6 2.3 %copy-start.2 = (bf16[384,8,256]{2,0,1:T(8,128)(2,1)S(1)}, bf16[384,8,256]{2,0,1:T(8,128)(2,1)}, u32[]{:S(2)}) copy-start(bf16[384,8,256]{2,0,1:T(8,128)(2,1)} %copy-done.1) | copy-start | bytes 4718596
  145.6 2.3 %copy-start.5 = (f32[8,64,256]{2,1,0:T(8,128)S(1)}, f32[8,64,256]{2,1,0:T(8,128)}, u32[]{:S(2)}) copy-start(f32[8,64,256]{2,1,0:T(8,128)} %all-reduce.3.cloned.1.call-done) | copy-start | bytes 1572868
  147.9 1.2 copy-start.16
Sparse Core Ops, SparseCore 0:
  75.9 69.6 all-reduce.2
  150.8 7.5 reduce-scatter.1
where the time goes:
time: 168 us; the launch traced here: 167 us
  waiting for transfers between devices  73.7 us (44%)
  blocking collectives  24.6 us (15%)
  matrix products  19.5 us (12%)
  between operations  13.7 us (8%)
  local copies, waits for them, and re-layouts  13 us (8%)
  starting transfers between devices  11.8 us (7%)
  other arithmetic  10.9 us (6%)
    psum x1, waiting for transfers between devices, shards(): kv_state, normalizer = lax.psum((state, key_sum), ('tile', 'col'))  60.6 us
    psum x1, blocking collectives, shards(): kv_state, normalizer = lax.psum((state, key_sum), ('tile', 'col'))  19.8 us
    dot_general x2, matrix products, features(): jnp.einsum('the,me->thm', scaled, omega, precision=lax.Precision.HIGHEST)  10.1 us
    ppermute x2, starting transfers between devices, extended(): lax.ppermute(tail, axis, [(i, (i + 1) % count) for i in range(ends)])  9.05 us
    reduce_scatter x1, waiting for transfers between devices, shards(): lax.psum_scatter(lax.dot_general(out_weight, attended, (((0,), (1,)), (()...  7.69 us
    ppermute x2, waiting for transfers between devices, extended(): lax.ppermute(head, axis, [((i + 1) % count, i) for i in range(ends)])  5.17 us
  transfers between devices with their start and end apart: 6, of which 5 were waited for; matrix products, arithmetic and copies ran while one was open for 8% of the time, Pallas kernels for 0%

commit v1 on v0

--- a/solution.py
+++ b/solution.py
@@ -73,7 +73,7 @@
     value_part = projected[2].reshape(tokens, heads_here, E)
     state = jnp.einsum("the,thm->hem", value_part, key_feat, preferred_element_type=jnp.float32)
     key_sum = jnp.sum(key_feat.astype(jnp.float32), axis=0)
-    kv_state, normalizer = lax.psum((state, key_sum), ("tile", "col"))
+    kv_state, normalizer = lax.psum(lax.psum((state, key_sum), "col"), "tile")
     query_part = projected[0].astype(jnp.float32).reshape(tokens, heads_here, E) * scale
     query_feat = features(query_part, omega)
     state_upper, state_lower = split_pair(kv_state)

time: 168 us -> 162 us (0.964)
  blocking collectives: 24.6 us -> 20.1 us
  waiting for transfers between devices: 73.7 us -> 69.7 us
  matrix products: 19.5 us -> 22.2 us
    psum x1 -> x2, waiting for transfers between devices: 60.6 us -> 55.8 us  [shards(): kv_state, normalizer = lax.psum(lax.psum((state, key_sum), 'col'), 'tile')]
    psum x1 -> x2, blocking collectives: 19.8 us -> 15.2 us  [shards(): kv_state, normalizer = lax.psum(lax.psum((state, key_sum), 'col'), 'tile')]
  transfers between devices with their start and end apart: 6 -> 7, of which waited for: 5 -> 6; matrix products, arithmetic and copies ran while one was open for 8% -> 10% of each run, Pallas kernels for 0% -> 0%
where the time goes in v1:
time: 162 us; the launch traced here: 161 us
  waiting for transfers between devices  69.7 us (43%)
  matrix products  22.2 us (14%)
  blocking collectives  20.1 us (12%)
  between operations  13.4 us (8%)
  local copies, waits for them, and re-layouts  12.9 us (8%)
  starting transfers between devices  11.7 us (7%)
  other arithmetic  10.9 us (7%)
    psum x2, waiting for transfers between devices, shards(): kv_state, normalizer = lax.psum(lax.psum((state, key_sum), 'col'), 'tile')  55.8 us
    psum x2, blocking collectives, shards(): kv_state, normalizer = lax.psum(lax.psum((state, key_sum), 'col'), 'tile')  15.2 us
    dot_general x2, matrix products, features(): jnp.einsum('the,me->thm', scaled, omega, precision=lax.Precision.HIGHEST)  11.3 us
    ppermute x2, starting transfers between devices, extended(): lax.ppermute(tail, axis, [(i, (i + 1) % count) for i in range(ends)])  9.04 us
    reduce_scatter x1, waiting for transfers between devices, shards(): lax.psum_scatter(lax.dot_general(out_weight, attended, (((0,), (1,)), (()...  8.39 us
    ppermute x2, waiting for transfers between devices, extended(): lax.ppermute(head, axis, [((i + 1) % count, i) for i in range(ends)])  5.18 us
  transfers between devices with their start and end apart: 7, of which 6 were waited for; matrix products, arithmetic and copies ran while one was open for 10% of the time, Pallas kernels for 0%

profile of v1, /device:TPU:0, one launch (start us, length us, event | category | flops | bytes accessed | tf_op | source)
XLA Modules:
  0.0 160.8 jit_solution(10050955853520850819)
XLA Ops:
  7.5 5.0 %collective-permute-start = (bf16[1,24,512]{2,1,0:T(8,128)(2,1)S(1)}, bf16[1,24,512]{2,1,0:T(8,128)(2,1)S(1)}, u32[]{:S(2)}, u32[]{:S(2)}) collective-permute-start(bf16[1,24,512]{2,1,0:T(8,128)(2,1)S(1)} %get-tuple-element.15), channel_id=1, source_target_pairs={{0,4},{4,8},{8,12},{1,5},{5,9},{9,13},{2,6},{6,10},{10,14},{3,7},{... | collective-permute-start | bytes 73736 | tf_op jit(solution)/shard_map/ppermute | solution.py:19
  15.0 3.2 %collective-permute-done.1 = bf16[1,24,512]{2,1,0:T(8,128)(2,1)S(1)} collective-permute-done((bf16[1,24,512]{2,1,0:T(8,128)(2,1)S(1)}, bf16[1,24,512]{2,1,0:T(8,128)(2,1)S(1)}, u32[]{:S(2)}, u32[]{:S(2)}) %collective-permute-start.1) | collective-permute-done | bytes 24608 | tf_op jit(solution)/shard_map/ppermute | solution.py:21
  19.7 4.0 %collective-permute-start.2 = (bf16[18,1,512]{2,1,0:T(2,128)(2,1)}, bf16[18,1,512]{2,1,0:T(2,128)(2,1)}, u32[]{:S(2)}, u32[]{:S(2)}) collective-permute-start(bf16[18,1,512]{2,1,0:T(2,128)(2,1)} %get-tuple-element.12), channel_id=1, source_target_pairs={{0,2},{1,3},{4,6},{5,7},{8,10},{9,11},{12,14},{13,15},{16,18},{17,... | collective-permute-start | bytes 55304 | tf_op jit(solution)/shard_map/ppermute | solution.py:19
  25.0 1.5 fusion.35
  27.8 2.0 %collective-permute-done.3 = bf16[18,1,512]{2,1,0:T(2,128)(2,1)} collective-permute-done((bf16[18,1,512]{2,1,0:T(2,128)(2,1)}, bf16[18,1,512]{2,1,0:T(2,128)(2,1)}, u32[]{:S(2)}, u32[]{:S(2)}) %collective-permute-start.3) | collective-permute-done | bytes 18464 | tf_op jit(solution)/shard_map/ppermute | solution.py:21
  31.2 1.7 %fusion.31 = (f32[16,24]{1,0:T(8,128)S(1)}, f32[16,24]{1,0:T(8,128)S(1)}, f32[16,24,512]{2,1,0:T(8,128)}) fusion(f32[18,26,512]{2,1,0:T(8,128)S(1)} %maximum_convert_fusion, f32[512]{0:T(512)S(1)} %bitcast.83, f32[512]{0:T(512)S(1)} %bitcast.82, f32[512]{0:T(512)S(1)} %bitcast.81, f32[512]{0:T(512)S(1)} %bitcast.80, f32[512]{0:T(512)S(1)} %bitcast.79, ...), kind=kLoop, calls=%fused_computation.65 | loop fusion | flops 4324608 | bytes 8279040 | tf_op jit(solution)/shard_map/reduce_sum | solution.py:55
  33.1 2.5 %all-reduce = (f32[384]{0:T(512)S(1)}, f32[384]{0:T(512)S(1)}) all-reduce(f32[384]{0:T(512)S(1)} %reduce_sum.52, f32[384]{0:T(512)S(1)} %reduce_sum.50), channel_id=1, replica_groups=mesh['slides'=2,'tile'=4,'col'=2,'mp'=2] {'mp'}, use_global_device_ids=true, to_apply=%region_3.0 | all-reduce | flops 768 | bytes 6144 | tf_op jit(solution)/shard_map/psum | solution.py:55
  36.9 2.4 %all_gather.3 = bf16[384,1024]{1,0:T(8,128)(2,1)S(1)} all-gather(bf16[384,512]{1,0:T(8,128)(2,1)S(1)} %fusion.19), channel_id=1, replica_groups=mesh['slides'=2,'tile'=4,'col'=2,'mp'=2] {'mp'}, dimensions={1}, use_global_device_ids=true | all-gather | bytes 1179648 | tf_op jit(solution)/shard_map/all_gather | solution.py:64
  39.3 1.4 fusion.1
  41.5 1.4 convert_multiply_fusion.1
  44.0 2.3 %copy.12 = f32[1,384,512]{1,2,0:T(8,128)} copy(f32[1,384,512]{2,1,0:T(8,128)} %get-tuple-element.10) | data formatting | bytes 1572864 | tf_op jit(solution)/shard_map/mul | solution.py:70
  47.6 5.8 %convert_reduce_fusion = (f32[8,256]{1,0:T(8,128)S(1)}, bf16[384,8,256]{2,0,1:T(8,128)(2,1)}) fusion(bf16[384]{0:T(512)(128)(2,1)S(1)} %copy-done.15, f32[384,8]{0,1:T(8,128)S(1)} %broadcast_multiply_fusion.1, f32[384,8,64]{0,2,1:T(8,128)} %bitcast.71, f32[256,64]{0,1:T(8,128)} %param.12), kind=kOutput, calls=%fused_computation | convolution fusion | flops 608696320 | bytes 2446080 | tf_op jit(solution)/shard_map/the,me->thm/dot_general | solution.py:29
  53.3 5.0 %psum.46 = f32[8,256]{1,0:T(8,128)S(1)} all-reduce(f32[8,256]{1,0:T(8,128)S(1)} %get-tuple-element.29), channel_id=1, replica_groups=mesh['slides'=2,'tile'=4,'col'=2,'mp'=2] {'col'}, use_global_device_ids=true, to_apply=%region_9.0 | all-reduce | flops 2048 | bytes 16384 | tf_op jit(solution)/shard_map/psum | solution.py:76
  58.3 10.3 %psum.47 = f32[8,256]{1,0:T(8,128)S(1)} all-reduce(f32[8,256]{1,0:T(8,128)S(1)} %psum.46), channel_id=1, replica_groups=mesh['slides'=2,'tile'=4,'col'=2,'mp'=2] {'tile'}, use_global_device_ids=true, to_apply=%region_10.0 | all-reduce | flops 2048 | bytes 16384 | tf_op jit(solution)/shard_map/psum | solution.py:76
  68.5 2.6 %fusion.36 = f32[8,64,256]{2,1,0:T(8,128)} fusion(bf16[384,8,64]{0,2,1:T(8,128)(2,1)S(1)} %bitcast.74, bf16[384,8,256]{2,0,1:T(8,128)(2,1)} %get-tuple-element.30), kind=kOutput, calls=%fused_computation.69 | convolution fusion | flops 100663296 | bytes 2490368 | tf_op jit(solution)/shard_map/the,thm->hem/dot_general | solution.py:74
  71.2 2.3 %copy.13 = f32[1,384,512]{1,2,0:T(8,128)} copy(f32[1,384,512]{2,1,0:T(8,128)} %get-tuple-element.11) | data formatting | bytes 1572864 | tf_op jit(solution)/shard_map/mul | solution.py:77
  74.8 5.5 %multiply_convert_fusion = bf16[384,8,256]{2,0,1:T(8,128)(2,1)} fusion(f32[384,8,64]{0,2,1:T(8,128)} %bitcast.73, f32[384,8]{0,1:T(8,128)S(1)} %broadcast_multiply_fusion, f32[256,64]{0,1:T(8,128)S(1)} %copy-done.17), kind=kOutput, calls=%fused_computation.1 | convolution fusion | flops 606339072 | bytes 2437120 | tf_op jit(solution)/shard_map/the,me->thm/dot_general | solution.py:29
  80.3 17.7 %all-reduce.4.cloned.1.call-done = f32[8,64,256]{2,1,0:T(8,128)} async-done(((f32[8,64,256]{2,1,0:T(8,128)}), f32[8,64,256]{2,1,0:T(8,128)}) %all-reduce.4.cloned.1.call-update) | async-done | bytes 524304 | tf_op jit(solution)/shard_map/psum | solution.py:76
  98.0 2.0 %fusion.26 = f32[8,1,384]{2,1,0:T(1,128)S(1)} fusion(bf16[384,8,256]{2,0,1:T(8,128)(2,1)} %multiply_convert_fusion, bf16[8,256,1]{1,0,2:T(8,128)(2,1)S(1)} %get-tuple-element.26), kind=kOutput, calls=%fused_computation.54 | convolution fusion | flops 1572864 | bytes 1589248 | tf_op jit(solution)/shard_map/thm,hm->th/dot_general | solution.py:86
  100.6 38.2 %all-reduce.6.cloned.1.call-done = f32[8,64,256]{2,1,0:T(8,128)} async-done(((f32[8,64,256]{2,1,0:T(8,128)}), f32[8,64,256]{2,1,0:T(8,128)}) %all-reduce.6.cloned.1.call-update) | async-done | bytes 524304 | tf_op jit(solution)/shard_map/psum | solution.py:76
  138.8 2.3 %fusion.21 = f32[8,64,384]{2,1,0:T(8,128)S(1)} fusion(bf16[384,8,256]{2,0,1:T(8,128)(2,1)} %multiply_convert_fusion, f32[8,64,256]{2,1,0:T(8,128)} %all-reduce.6.cloned.1.call-done), kind=kOutput, calls=%fused_computation.45 | convolution fusion | flops 100794368 | bytes 2883584 | tf_op jit(solution)/shard_map/thm,hem->the/dot_general | solution.py:81
  142.3 1.5 fusion.2
  143.8 8.4 %reduce-scatter.2.cloned.1.call-done = bf16[512,384]{0,1:T(8,128)(2,1)} async-done(((bf16[1024,384]{0,1:T(8,128)(2,1)}), bf16[512,384]{0,1:T(8,128)(2,1)}) %reduce-scatter.2.cloned.1.call-update) | async-done | bytes 393232 | tf_op jit(solution)/shard_map/reduce_scatter | solution.py:91
  152.2 2.1 %fusion.15 = bf16[384,512]{1,0:T(8,128)(2,1)} fusion(f32[16,24,512]{2,1,0:T(8,128)} %get-tuple-element.9, bf16[512,384]{0,1:T(8,128)(2,1)} %reduce-scatter.2.cloned.1.call-done), kind=kLoop, calls=%fused_computation.31 | loop fusion | flops 589824 | bytes 1572864 | tf_op jit(solution)/shard_map/convert_element_type | solution.py:102
  (68 shorter events, 16.6 us)
Async XLA Ops:
  6.5 32.7 %copy-start = (bf16[3,1024,512]{2,1,0:T(8,128)(2,1)S(1)}, bf16[3,1024,512]{2,1,0:T(8,128)(2,1)}, u32[]{:S(2)}) copy-start(bf16[3,1024,512]{2,1,0:T(8,128)(2,1)} %param.11) | copy-start | bytes 9437188
  6.5 24.6 %copy-start.3 = (bf16[16,24,512]{2,1,0:T(8,128)(2,1)S(1)}, bf16[16,24,512]{2,1,0:T(8,128)(2,1)}, u32[]{:S(2)}) copy-start(bf16[16,24,512]{2,1,0:T(8,128)(2,1)} %param.7) | copy-start | bytes 1179652
  6.5 91.4 %all-reduce.4.cloned.1.call-start = ((), (), s32[]{:S(2)}) async-start(), calls=%async_computation.1 | async-start | bytes 1048576 | tf_op jit(solution)/shard_map/psum | solution.py:76
  7.5 6.6 %collective-permute-start = (bf16[1,24,512]{2,1,0:T(8,128)(2,1)S(1)}, bf16[1,24,512]{2,1,0:T(8,128)(2,1)S(1)}, u32[]{:S(2)}, u32[]{:S(2)}) collective-permute-start(bf16[1,24,512]{2,1,0:T(8,128)(2,1)S(1)} %get-tuple-element.15), channel_id=1, source_target_pairs={{0,4},{4,8},{8,12},{1,5},{5,9},{9,13},{2,6},{6,10},{10,14},{3,7},{... | collective-permute-start | bytes 73736 | tf_op jit(solution)/shard_map/ppermute | solution.py:19
  12.5 5.7 %collective-permute-start.1 = (bf16[1,24,512]{2,1,0:T(8,128)(2,1)S(1)}, bf16[1,24,512]{2,1,0:T(8,128)(2,1)S(1)}, u32[]{:S(2)}, u32[]{:S(2)}) collective-permute-start(bf16[1,24,512]{2,1,0:T(8,128)(2,1)S(1)} %get-tuple-element.14), channel_id=1, source_target_pairs={{4,0},{8,4},{12,8},{5,1},{9,5},{13,9},{6,2},{10,6},{14,10},{7,3},{... | collective-permute-start | bytes 73736 | tf_op jit(solution)/shard_map/ppermute | solution.py:21
  19.7 8.2 %collective-permute-start.2 = (bf16[18,1,512]{2,1,0:T(2,128)(2,1)}, bf16[18,1,512]{2,1,0:T(2,128)(2,1)}, u32[]{:S(2)}, u32[]{:S(2)}) collective-permute-start(bf16[18,1,512]{2,1,0:T(2,128)(2,1)} %get-tuple-element.12), channel_id=1, source_target_pairs={{0,2},{1,3},{4,6},{5,7},{8,10},{9,11},{12,14},{13,15},{16,18},{17,... | collective-permute-start | bytes 55304 | tf_op jit(solution)/shard_map/ppermute | solution.py:19
  23.7 6.2 %collective-permute-start.3 = (bf16[18,1,512]{2,1,0:T(2,128)(2,1)}, bf16[18,1,512]{2,1,0:T(2,128)(2,1)}, u32[]{:S(2)}, u32[]{:S(2)}) collective-permute-start(bf16[18,1,512]{2,1,0:T(2,128)(2,1)} %get-tuple-element.13), channel_id=1, source_target_pairs={{2,0},{3,1},{6,4},{7,5},{10,8},{11,9},{14,12},{15,13},{18,16},{19,... | collective-permute-start | bytes 55304 | tf_op jit(solution)/shard_map/ppermute | solution.py:21
  27.8 3.3 %copy-start.6 = (f32[1,1,512]{2,1,0:T(1,128)S(1)}, f32[1,1,512]{2,1,0:T(1,128)}, u32[]{:S(2)}) copy-start(f32[1,1,512]{2,1,0:T(1,128)} %get-tuple-element.16) | copy-start | bytes 6148
  27.8 3.3 %copy-start.7 = (f32[1,1,512]{2,1,0:T(1,128)S(1)}, f32[1,1,512]{2,1,0:T(1,128)}, u32[]{:S(2)}) copy-start(f32[1,1,512]{2,1,0:T(1,128)} %get-tuple-element.17) | copy-start | bytes 6148
  27.8 3.3 %copy-start.8 = (f32[1,1,512]{2,1,0:T(1,128)S(1)}, f32[1,1,512]{2,1,0:T(1,128)}, u32[]{:S(2)}) copy-start(f32[1,1,512]{2,1,0:T(1,128)} %get-tuple-element.18) | copy-start | bytes 6148
  27.8 3.4 %copy-start.9 = (f32[1,1,512]{2,1,0:T(1,128)S(1)}, f32[1,1,512]{2,1,0:T(1,128)}, u32[]{:S(2)}) copy-start(f32[1,1,512]{2,1,0:T(1,128)} %get-tuple-element.19) | copy-start | bytes 6148
  27.8 3.4 %copy-start.10 = (f32[1,1,512]{2,1,0:T(1,128)S(1)}, f32[1,1,512]{2,1,0:T(1,128)}, u32[]{:S(2)}) copy-start(f32[1,1,512]{2,1,0:T(1,128)} %get-tuple-element.20) | copy-start | bytes 6148
  27.8 3.4 %copy-start.11 = (f32[1,1,512]{2,1,0:T(1,128)S(1)}, f32[1,1,512]{2,1,0:T(1,128)}, u32[]{:S(2)}) copy-start(f32[1,1,512]{2,1,0:T(1,128)} %get-tuple-element.21) | copy-start | bytes 6148
  27.8 3.4 %copy-start.12 = (f32[1,1,512]{2,1,0:T(1,128)S(1)}, f32[1,1,512]{2,1,0:T(1,128)}, u32[]{:S(2)}) copy-start(f32[1,1,512]{2,1,0:T(1,128)} %get-tuple-element.22) | copy-start | bytes 6148
  27.8 3.4 %copy-start.13 = (f32[1,1,512]{2,1,0:T(1,128)S(1)}, f32[1,1,512]{2,1,0:T(1,128)}, u32[]{:S(2)}) copy-start(f32[1,1,512]{2,1,0:T(1,128)} %get-tuple-element.23) | copy-start | bytes 6148
  27.8 3.4 %copy-start.14 = (f32[1,1,512]{2,1,0:T(1,128)S(1)}, f32[1,1,512]{2,1,0:T(1,128)}, u32[]{:S(2)}) copy-start(f32[1,1,512]{2,1,0:T(1,128)} %get-tuple-element.24) | copy-start | bytes 6148
  42.8 4.7 %copy-start.15 = (bf16[384]{0:T(512)(128)(2,1)S(1)}, bf16[384]{0:T(512)(128)(2,1)}, u32[]{:S(2)}) copy-start(bf16[384]{0:T(512)(128)(2,1)} %convert_element_type.95) | copy-start | bytes 2308
  71.2 3.6 %copy-start.17 = (f32[256,64]{0,1:T(8,128)S(1)}, f32[256,64]{0,1:T(8,128)}, u32[]{:S(2)}) copy-start(f32[256,64]{0,1:T(8,128)} %param.12) | copy-start | bytes 196612
  71.2 67.6 %all-reduce.6.cloned.1.call-start = ((), (), s32[]{:S(2)}) async-start(), calls=%async_computation.2 | async-start | bytes 1048576 | tf_op jit(solution)/shard_map/psum | solution.py:76
  98.0 54.2 %reduce-scatter.2.cloned.1.call-start = ((), (), s32[]{:S(2)}) async-start(), calls=%async_computation.3 | async-start | bytes 1179648 | tf_op jit(solution)/shard_map/reduce_scatter | solution.py:91
  98.0 2.0 %copy-start.1 = (bf16[384,8,256]{2,0,1:T(8,128)(2,1)S(1)}, bf16[384,8,256]{2,0,1:T(8,128)(2,1)}, u32[]{:S(2)}) copy-start(bf16[384,8,256]{2,0,1:T(8,128)(2,1)} %multiply_convert_fusion) | copy-start | bytes 4718596
  138.8 2.3 %copy-start.2 = (bf16[384,8,256]{2,0,1:T(8,128)(2,1)S(1)}, bf16[384,8,256]{2,0,1:T(8,128)(2,1)}, u32[]{:S(2)}) copy-start(bf16[384,8,256]{2,0,1:T(8,128)(2,1)} %multiply_convert_fusion) | copy-start | bytes 4718596
  138.8 2.3 %copy-start.5 = (f32[8,64,256]{2,1,0:T(8,128)S(1)}, f32[8,64,256]{2,1,0:T(8,128)}, u32[]{:S(2)}) copy-start(f32[8,64,256]{2,1,0:T(8,128)} %all-reduce.6.cloned.1.call-done) | copy-start | bytes 1572868
  141.1 1.2 copy-start.16
  (1 other events, 0.8 us)
Sparse Core Ops, SparseCore 0:
  71.3 26.5 all-reduce.3
  100.4 38.2 all-reduce.5
  143.9 8.2 reduce-scatter.1
